TPU v7x, 256 devices: a whole 4x4x8 slice. The times are simulated.
256 devices in a mesh: dom: 32 (over z, y), feat: 8 (over x, core).
Axes of the slice: x: 4, y: 4, z: 8, core: 2. Of those that a mesh axis runs over, the one named last changes fastest.
Arguments:
- features: bfloat16 [8192, 8, 25088], P('dom', 'feat'), may hold values from -50 to 50, as said below
- weights: float32 [8, 32, 25088], P('feat', None, 'dom'), may hold values from -6 to 6
- geno_live: int32 [4], replicated, may hold values from 1 to 25088, 100000 in all
- image_live: int32 [4], replicated, may hold values from 1 to 12544, 50000 in all
Outputs:
- updated: float32 [8, 32, 25088], P('feat', None, 'dom')
Inputs may be any that keep to these rules, and one draw needn't show every extreme that they name: `features`: rows are participants; every entry is finite. `geno_live`: the counts sum to 100000. `image_live`: the counts sum to 50000.
All inputs are finite; a program needn't handle non-finite values.
Results may differ from a plain program's by a relative error of at most 0.0048.
Values may be sent and summed in bfloat16 or wider, within the bound.
No kernel may reach another device: no remote copies, remote signals or barrier semaphores. Data moves between devices by JAX's collectives and lax.ppermute only.
A program may use at most 64 MiB of HBM per device.

v0:
```python
import jax
import jax.numpy as jnp
from jax import lax
from jax.sharding import PartitionSpec as P

GX = 100000
GY = 50000
K = 32
ITERS = 2


step_rate = 0.1
jitter = 1e-05


def body(features, weights, geno_live, image_live):
    row_count = features.shape[0]
    own_block = features[:, 0, :]
    shard_width = weights.shape[2]
    participants = row_count * lax.axis_size("dom")
    half_feat = lax.axis_size("feat") // 2
    feat_index = lax.axis_index("feat")
    is_geno = feat_index < half_feat
    block_slot = feat_index % half_feat
    live_count = jnp.where(
        is_geno,
        lax.dynamic_index_in_dim(geno_live, block_slot, 0, False),
        lax.dynamic_index_in_dim(image_live, block_slot, 0, False),
    )
    offset = lax.axis_index("dom") * shard_width
    mask_own = (lax.iota(jnp.int32, shard_width) + offset < live_count).astype(jnp.float32)
    step_size = step_rate * participants ** (-0.5)
    identity = jnp.eye(K, dtype=jnp.float32)
    current = weights
    for sweep in range(ITERS):
        rounded = (current * mask_own).astype(jnp.bfloat16)
        partial_value = lax.dot_general(
            own_block,
            lax.all_gather(rounded, "dom", axis=2, tiled=True)[0],
            (((1,), (1,)), ((), ())),
            preferred_element_type=jnp.float32,
        )
        zero_part = jnp.zeros_like(partial_value)
        stacked = jnp.where(
            is_geno, jnp.stack([partial_value, zero_part]), jnp.stack([zero_part, partial_value])
        )
        view_totals = lax.psum(stacked, "feat")
        geno_proj = view_totals[0] * GX ** (-0.5)
        image_proj = view_totals[1] * GY ** (-0.5)
        projected = jnp.stack([geno_proj, image_proj])
        local_gram = jnp.einsum(
            "vrk,vrl->vkl", projected, projected, precision=lax.Precision.HIGHEST
        )
        gram_total = lax.psum(local_gram, "dom")
        factor = jnp.linalg.cholesky(gram_total / participants + jitter * identity)
        own_proj = jnp.where(is_geno, geno_proj, image_proj)
        partner = jnp.where(is_geno, image_proj, geno_proj)
        partner_factor = jnp.where(is_geno, factor[1], factor[0])
        target = jax.scipy.linalg.solve_triangular(partner_factor, partner.T, lower=True).T
        residual_rows = (own_proj - target).astype(jnp.bfloat16)
        full_term = lax.dot_general(
            own_block, residual_rows, (((0,), (0,)), ((), ())), preferred_element_type=jnp.float32
        )
        share = lax.psum_scatter(full_term, "dom", scatter_dimension=0, tiled=True)
        gradient = share.T[None]
        current = mask_own * (current - step_size * gradient)
    return current


def solution(mesh):
    placed = (P("dom", "feat", None), P("feat", None, "dom"), P(), P())
    return jax.shard_map(
        body, mesh=mesh, in_specs=placed, out_specs=P("feat", None, "dom"), check_vma=False
    )
```

profile of v0, /device:TPU:8, one launch (start us, length us, event | category | flops | bytes accessed | tf_op | source)
XLA Modules:
  0.0 1254.7 jit_solution(13057092313761580791)
XLA Ops:
  6.5 1.3 dynamic_slice.8
  7.9 1.2 dynamic_slice.7
  12.6 122.6 %all-gather.3.cloned.1.call-done = bf16[1,32,25088]{1,0,2:T(2,128)(2,1)} async-done(((bf16[1,32,784]{1,0,2:T(2,128)(2,1)}), bf16[1,32,25088]{1,0,2:T(2,128)(2,1)}) %all-gather.3.cloned.1.call-update) | async-done | bytes 1605648 | tf_op jit(solution)/shard_map/all_gather | solution.py:39
  135.2 23.1 %copy.56 = bf16[1,32,25088]{2,1,0:T(8,128)(2,1)S(1)} copy(bf16[1,32,25088]{1,0,2:T(2,128)(2,1)} %all-gather.3.cloned.1.call-done) | data formatting | bytes 3211264 | tf_op jit(solution)/shard_map/all_gather | solution.py:39
  158.3 8.4 fusion.8
  167.5 62.2 %all-reduce.7.cloned.1.call-done = f32[2,256,32]{1,2,0:T(8,128)} async-done(((f32[2,256,32]{1,2,0:T(8,128)}), f32[2,256,32]{1,2,0:T(8,128)}) %all-reduce.7.cloned.1.call-update) | async-done | bytes 65552 | tf_op jit(solution)/shard_map/psum | solution.py:47
  230.6 138.1 %psum.29 = f32[2,32,32]{1,2,0:T(8,128)S(1)} all-reduce(f32[2,32,32]{1,2,0:T(8,128)S(1)} %fusion.24), channel_id=1, replica_groups=mesh['dom'=32,'feat'=8] {'dom'}, use_global_device_ids=true, to_apply=%region_1.2 | all-reduce | flops 2048 | bytes 16384 | tf_op jit(solution)/shard_map/psum | solution.py:54
  368.8 5.9 custom-call.8
  374.9 2.4 custom-call.9
  378.5 7.0 convolution_bitcast_fusion.1
  385.4 6.9 copy.65
  392.4 237.5 %reduce-scatter.7.cloned.1.call-done = f32[784,32]{1,0:T(8,128)} async-done(((f32[25088,32]{1,0:T(8,128)}), f32[784,32]{1,0:T(8,128)}) %reduce-scatter.7.cloned.1.call-update) | async-done | bytes 100368
  629.9 1.2 copy.66
  632.3 119.2 %all-gather.5.cloned.1.call-done = bf16[1,32,25088]{1,0,2:T(2,128)(2,1)} async-done(((bf16[1,32,784]{1,0,2:T(2,128)(2,1)}), bf16[1,32,25088]{1,0,2:T(2,128)(2,1)}) %all-gather.5.cloned.1.call-update) | async-done | bytes 1605648 | tf_op jit(solution)/shard_map/all_gather | solution.py:39
  751.5 23.1 %copy.60 = bf16[1,32,25088]{2,1,0:T(8,128)(2,1)S(1)} copy(bf16[1,32,25088]{1,0,2:T(2,128)(2,1)} %all-gather.5.cloned.1.call-done) | data formatting | bytes 3211264 | tf_op jit(solution)/shard_map/all_gather | solution.py:39
  774.7 8.4 fusion.13
  783.8 62.2 %all-reduce.9.cloned.1.call-done = f32[2,256,32]{1,2,0:T(8,128)} async-done(((f32[2,256,32]{1,2,0:T(8,128)}), f32[2,256,32]{1,2,0:T(8,128)}) %all-reduce.9.cloned.1.call-update) | async-done | bytes 65552 | tf_op jit(solution)/shard_map/psum | solution.py:47
  846.9 138.1 %psum.31 = f32[2,32,32]{1,2,0:T(8,128)S(1)} all-reduce(f32[2,32,32]{1,2,0:T(8,128)S(1)} %fusion.28), channel_id=1, replica_groups=mesh['dom'=32,'feat'=8] {'dom'}, use_global_device_ids=true, to_apply=%region_6.9 | all-reduce | flops 2048 | bytes 16384 | tf_op jit(solution)/shard_map/psum | solution.py:54
  985.1 5.9 custom-call.10
  991.2 2.4 custom-call.11
  994.8 7.0 convolution_bitcast_fusion
  1001.7 6.9 copy.67
  1008.6 237.4 %reduce-scatter.9.cloned.1.call-done = f32[784,32]{1,0:T(8,128)} async-done(((f32[25088,32]{1,0:T(8,128)}), f32[784,32]{1,0:T(8,128)}) %reduce-scatter.9.cloned.1.call-update) | async-done | bytes 100368
  1246.0 1.2 copy.68
  (45 shorter events, 10.3 us)
Async XLA Ops:
  6.5 128.7 %all-gather.3.cloned.1.call-start = ((), (), s32[]{:S(2)}) async-start(), calls=%async_computation.2 | async-start | bytes 13246464 | tf_op jit(solution)/shard_map/all_gather | solution.py:39
  12.5 217.2 %all-reduce.7.cloned.1.call-start = ((), (), s32[]{:S(2)}) async-start(), calls=%async_computation.3 | async-start | bytes 131072 | tf_op jit(solution)/shard_map/psum | solution.py:47
  167.4 462.5 %reduce-scatter.7.cloned.1.call-start = ((), (), s32[]{:S(2)}) async-start(), calls=%async_computation.6 | async-start | bytes 13246464
  385.4 245.7 %copy-start = (f32[1,32,784]{2,1,0:T(8,128)S(1)}, f32[1,32,784]{2,1,0:T(8,128)}, u32[]{:S(2)}) copy-start(f32[1,32,784]{2,1,0:T(8,128)} %param.8) | copy-start | bytes 301060
  392.3 359.2 %all-gather.5.cloned.1.call-start = ((), (), s32[]{:S(2)}) async-start(), calls=%async_computation.4 | async-start | bytes 13246464 | tf_op jit(solution)/shard_map/all_gather | solution.py:39
  632.2 213.7 %all-reduce.9.cloned.1.call-start = ((), (), s32[]{:S(2)}) async-start(), calls=%async_computation.5 | async-start | bytes 131072 | tf_op jit(solution)/shard_map/psum | solution.py:47
  783.7 462.3 %reduce-scatter.9.cloned.1.call-start = ((), (), s32[]{:S(2)}) async-start(), calls=%async_computation.7 | async-start | bytes 13246464
Sparse Core Ops, SparseCore 0:
  12.6 122.5 all-gather.2
  167.5 62.0 all-reduce.6
  392.5 237.4 reduce-scatter.6
  632.7 118.8 all-gather.4
  783.8 62.0 all-reduce.8
  1008.7 237.2 reduce-scatter.8
where the time goes:
time: 1260 us; the launch traced here: 1250 us
  waiting for transfers between devices  841 us (67%)
  blocking collectives  276 us (22%)
  local copies, waits for them, and re-layouts  67.2 us (5%)
  matrix products  33.2 us (3%)
  other arithmetic  21.7 us (2%)
  between operations  14.9 us (1%)
    unnamed x8, waiting for transfers between devices  475 us
    psum x2, blocking collectives, body(): gram_total = lax.psum(local_gram, 'dom')  276 us
    all_gather x2, waiting for transfers between devices, body(): lax.all_gather(rounded, 'dom', axis=2, tiled=True)[0]  242 us
    psum x2, waiting for transfers between devices, body(): view_totals = lax.psum(stacked, 'feat')  124 us
    all_gather x2, local copies, waits for them, and re-layouts, body(): lax.all_gather(rounded, 'dom', axis=2, tiled=True)[0]  46.2 us
  transfers between devices with their start and end apart: 6, of which 6 were waited for; matrix products, arithmetic and copies ran while one was open for 0% of the time, Pallas kernels for 0%

commit v1 on v0

v1 whole, which is shorter than its diff:
```python
import functools
import jax
import jax.numpy as jnp
from jax import lax
from jax.experimental import pallas as pl
from jax.experimental.pallas import tpu as pltpu
from jax.sharding import PartitionSpec as P

GX = 100000
GY = 50000
K = 32
ITERS = 2
LANES = 128
step_rate = 0.1
jitter = 1e-05

VMEM = pl.BlockSpec(memory_space=pltpu.VMEM)
SMEM = pl.BlockSpec(memory_space=pltpu.SMEM)
PARAMS = pltpu.CompilerParams(vmem_limit_bytes=48 * 1024 * 1024)
HIGH = lax.Precision.HIGHEST
F32 = jnp.float32
BF16 = jnp.bfloat16


def window(width):
    return -(-(width + LANES - 16) // LANES) * LANES


def base_of(index, width):
    return (index * width) // LANES * LANES


def lane_mask(info, width):
    column = lax.broadcasted_iota(jnp.int32, (K, width), 1) + info[1] * width
    return (column < info[0]).astype(F32)


def spread(info, masked, width, pad, copies):
    pad[...] = jnp.zeros(pad.shape, F32)
    pad[:, :width] = masked
    shift = lax.rem(info[1] * width, LANES)
    rounded = pltpu.roll(pad[...], shift, 1).astype(BF16)
    for copy in range(copies.shape[0]):
        copies[copy] = rounded


def first_kernel(info, weights, copies, pad):
    width = weights.shape[1]
    spread(info, weights[...] * lane_mask(info, width), width, pad, copies)


def project_kernel(windows, features, copies, full):
    count, _, size = windows.shape
    width = features.shape[1] // count
    full[...] = jnp.zeros(full.shape, BF16)
    for shard in range(count):
        base = base_of(shard, width)
        full[:, base : base + size] += windows[shard]
    partial = lax.dot_general(
        features[...], full[...], (((1,), (1,)), ((), ())), preferred_element_type=F32
    ).T
    for copy in range(copies.shape[0]):
        copies[copy] = partial


def gram_kernel(info, partials, own, partner, copies):
    half = partials.shape[0] // 2
    geno = partials[0]
    image = partials[half]
    for block in range(1, half):
        geno += partials[block]
        image += partials[half + block]
    geno *= GX ** (-0.5)
    image *= GY ** (-0.5)
    is_geno = info[2] == 1
    own[...] = jnp.where(is_geno, geno, image)
    other = jnp.where(is_geno, image, geno)
    partner[...] = other
    tiled = jnp.concatenate([other] * (LANES // K), axis=0)
    gram = lax.dot_general(
        other, tiled, (((1,), (1,)), ((), ())), precision=HIGH, preferred_element_type=F32
    )
    lane = lax.broadcasted_iota(jnp.int32, (8, LANES), 1)
    packed = jnp.zeros((8, LANES), F32)
    for part in range(LANES // K):
        packed = jnp.where(lane // K == part, gram[8 * part : 8 * part + 8], packed)
    for copy in range(copies.shape[0]):
        copies[copy] = packed


def residual_kernel(participants, grams, own, partner, features, windows):
    total = grams[0]
    for part in range(1, grams.shape[0]):
        total += grams[part]
    rows = [total] + [pltpu.roll(total, LANES - K * part, 1) for part in range(1, LANES // K)]
    row = lax.broadcasted_iota(jnp.int32, (K, LANES), 0)
    lane = lax.broadcasted_iota(jnp.int32, (K, LANES), 1)
    covariance = jnp.concatenate(rows, axis=0) / participants
    covariance += jnp.where(lane == row, jitter, 0.0)
    state = jnp.where(lane < K, covariance, jnp.where(lane == row + K, 1.0, 0.0))
    pivots = jnp.zeros((K, 1), F32)
    for step in range(K):
        pivot_row = state[step : step + 1, :]
        column = state[:, step : step + 1]
        pivot = pivot_row[:, step : step + 1]
        pivots = jnp.where(row[:, :1] == step, pivot, pivots)
        ratio = jnp.where(row[:, :1] > step, column / pivot, 0.0)
        state = state - ratio * pivot_row
    scaled = state * lax.rsqrt(pivots)
    inverse = pltpu.roll(scaled, LANES - K, 1)[:, :K]
    target = lax.dot_general(
        inverse, partner[...], (((1,), (0,)), ((), ())), precision=HIGH, preferred_element_type=F32
    )
    residual = (own[...] - target).astype(BF16)
    count, _, size = windows.shape
    width = features.shape[1] // count
    for shard in range(count):
        base = base_of(shard, width)
        windows[shard] = lax.dot_general(
            residual,
            features[:, base : base + size],
            (((1,), (0,)), ((), ())),
            preferred_element_type=F32,
        ).astype(BF16)


def updated_weights(step_size, info, windows, weights):
    width = weights.shape[1]
    total = windows[0].astype(F32)
    for part in range(1, windows.shape[0]):
        total += windows[part].astype(F32)
    size = windows.shape[2]
    shift = lax.rem(size - lax.rem(info[1] * width, LANES), size)
    gradient = pltpu.roll(total, shift, 1)[:, :width]
    return lane_mask(info, width) * (weights[...] - step_size * gradient)


def update_kernel(step_size, info, windows, weights, updated, copies, pad):
    width = weights.shape[1]
    fresh = updated_weights(step_size, info, windows, weights)
    updated[...] = fresh
    spread(info, fresh, width, pad, copies)


def last_kernel(step_size, info, windows, weights, updated):
    updated[...] = updated_weights(step_size, info, windows, weights)


def call(kernel, outs, scratch=(), specs=None):
    shapes = tuple(jax.ShapeDtypeStruct(*out) for out in outs)
    return pl.pallas_call(
        kernel,
        out_shape=shapes,
        in_specs=specs,
        out_specs=tuple(VMEM for _ in shapes),
        scratch_shapes=list(scratch),
        compiler_params=PARAMS,
    )


def exchange(copies, axis):
    return lax.all_to_all(copies, axis, 0, 0, tiled=True)


def body(features, weights, geno_live, image_live):
    row_count = features.shape[0]
    own_block = features[:, 0, :]
    current = weights[0]
    width = current.shape[1]
    size = window(width)
    doms = lax.axis_size("dom")
    feats = lax.axis_size("feat")
    participants = row_count * doms
    half = feats // 2
    feat = lax.axis_index("feat")
    lives = jnp.concatenate([geno_live, image_live])
    live_count = jnp.sum(jnp.where(jnp.arange(feats) == feat, lives, 0))
    info = jnp.stack([live_count, lax.axis_index("dom"), (feat < half).astype(jnp.int32)])
    step_size = step_rate * participants ** (-0.5)

    pad = pltpu.VMEM((K, size), F32)
    spread_out = ((doms, K, size), BF16)
    (copies,) = call(first_kernel, [spread_out], [pad], [SMEM, VMEM])(info, current)
    for sweep in range(ITERS):
        (copies,) = call(
            project_kernel,
            [((feats, K, row_count), F32)],
            [pltpu.VMEM((K, own_block.shape[1]), BF16)],
            [VMEM, VMEM],
        )(exchange(copies, "dom"), own_block)
        own, partner, copies = call(
            gram_kernel,
            [((K, row_count), F32), ((K, row_count), F32), ((doms, 8, LANES), F32)],
            (),
            [SMEM, VMEM],
        )(info, exchange(copies, "feat"))
        (copies,) = call(
            functools.partial(residual_kernel, participants), [spread_out], (), [VMEM] * 4
        )(exchange(copies, "dom"), own, partner, own_block)
        shares = exchange(copies, "dom")
        if sweep < ITERS - 1:
            current, copies = call(
                functools.partial(update_kernel, step_size),
                [(current.shape, F32), spread_out],
                [pad],
                [SMEM, VMEM, VMEM],
            )(info, shares, current)
        else:
            (current,) = call(
                functools.partial(last_kernel, step_size),
                [(current.shape, F32)],
                (),
                [SMEM, VMEM, VMEM],
            )(info, shares, current)
    return current[None]


def solution(mesh):
    placed = (P("dom", "feat", None), P("feat", None, "dom"), P(), P())
    return jax.shard_map(
        body, mesh=mesh, in_specs=placed, out_specs=P("feat", None, "dom"), check_vma=False
    )
```

time: 1260 us -> 296 us (0.23)
  waiting for transfers between devices: 841 us -> 0 us
  local copies, waits for them, and re-layouts: 67.2 us -> 0.91 us
  Pallas kernels: 0 us -> 40.9 us
  matrix products: 33.2 us -> 0 us
  blocking collectives: 276 us -> 252 us
  other arithmetic: 21.7 us -> 2.09 us
  between operations: 14.9 us -> 0.07 us
    unnamed x8 -> x0, waiting for transfers between devices: 475 us -> none
    psum x2 -> x0, blocking collectives: 276 us -> none  [body(): gram_total = lax.psum(local_gram, 'dom')]
    all_to_all x0 -> x8, blocking collectives: none -> 252 us  [exchange(): return lax.all_to_all(copies, axis, 0, 0, tiled=True)]
    all_gather x2 -> x0, waiting for transfers between devices: 242 us -> none  [body(): lax.all_gather(rounded, 'dom', axis=2, tiled=True)[0]]
    psum x2 -> x0, waiting for transfers between devices: 124 us -> none  [body(): view_totals = lax.psum(stacked, 'feat')]
    all_gather x2 -> x0, local copies, waits for them, and re-layouts: 46.2 us -> none  [body(): lax.all_gather(rounded, 'dom', axis=2, tiled=True)[0]]
    pallas_call x0 -> x9, Pallas kernels: none -> 40.9 us  [the longest x2 19.3 us: body(): call(functools.partial(residual_kernel, participants), [spread_out], (),...]
    dot_general x6 -> x0, matrix products: 31 us -> none  [the longest x2 16.7 us: body(): lax.dot_general(own_block, lax.all_gather(rounded, 'dom', axis=2, tiled=T...]
  transfers between devices with their start and end apart: 6 -> 0, of which waited for: 6 -> 0; matrix products, arithmetic and copies ran while one was open for 0% -> 0% of each run, Pallas kernels for 0% -> 0%
where the time goes in v1:
time: 296 us
  blocking collectives  252 us (85%)
  Pallas kernels  40.9 us (14%)
    all_to_all x8, blocking collectives, exchange(): return lax.all_to_all(copies, axis, 0, 0, tiled=True)  252 us
    pallas_call x2, Pallas kernels, body(): call(functools.partial(residual_kernel, participants), [spread_out], (),...  19.3 us
    pallas_call x2, Pallas kernels, body(): call(project_kernel, [((feats, K, row_count), F32)], [pltpu.VMEM((K, own_...  16.6 us

profile of v1, /device:TPU:8, one launch (start us, length us, event | category | flops | bytes accessed | tf_op | source)
XLA Modules:
  0.0 295.9 jit_solution(13311265387186421845)
XLA Ops:
  0.0 1.4 fusion
  1.4 0.7 pad_add_fusion.info
  2.1 0.0 copy-start
  2.1 0.9 copy-done
  3.0 0.8 shard_map.46
  3.8 56.4 %all_to_all.40.windows = bf16[32,32,896]{2,1,0:T(8,128)(2,1)S(1)} all-to-all(bf16[32,32,896]{2,1,0:T(8,128)(2,1)S(1)} %shard_map.46), channel_id=1, replica_groups=mesh['dom'=32,'feat'=8] {'dom'}, dimensions={0} | all-to-all | bytes 3670016 | tf_op jit(solution)/shard_map/all_to_all | solution.py:162
  60.2 8.3 %shard_map.47 = f32[8,32,256]{2,1,0:T(8,128)S(1)} custom-call(bf16[32,32,896]{2,1,0:T(8,128)(2,1)S(1)} %all_to_all.40.windows, bf16[256,25088]{1,0:T(8,128)(2,1)} %bitcast.8), custom_call_target="tpu_custom_call" | custom-call | tf_op jit(solution)/shard_map/pallas_call | solution.py:185
  68.5 11.6 %all_to_all.41.partials = f32[8,32,256]{2,1,0:T(8,128)S(1)} all-to-all(f32[8,32,256]{2,1,0:T(8,128)S(1)} %shard_map.47), channel_id=1, replica_groups=mesh['dom'=32,'feat'=8] {'feat'}, dimensions={0} | all-to-all | bytes 524288 | tf_op jit(solution)/shard_map/all_to_all | solution.py:162
  80.1 0.8 shard_map.48
  80.9 14.2 %all_to_all.42.grams = f32[32,8,128]{2,1,0:T(8,128)S(1)} all-to-all(f32[32,8,128]{2,1,0:T(8,128)S(1)} %get-tuple-element.13), channel_id=1, replica_groups=mesh['dom'=32,'feat'=8] {'dom'}, dimensions={0} | all-to-all | bytes 262144 | tf_op jit(solution)/shard_map/all_to_all | solution.py:162
  95.2 9.7 %shard_map.49 = bf16[32,32,896]{2,1,0:T(8,128)(2,1)S(1)} custom-call(f32[32,8,128]{2,1,0:T(8,128)S(1)} %all_to_all.42.grams, f32[32,256]{1,0:T(8,128)S(1)} %get-tuple-element.14.own, f32[32,256]{1,0:T(8,128)S(1)} %get-tuple-element.15.partner, bf16[256,25088]{1,0:T(8,128)(2,1)} %bitcast.9), custom_call_target="tpu_custom_call" | custom-call | tf_op jit(solution)/shard_map/pallas_call | solution.py:197
  104.8 0.0 copy-start.1
  104.8 48.5 %all_to_all.43.windows = bf16[32,32,896]{2,1,0:T(8,128)(2,1)S(1)} all-to-all(bf16[32,32,896]{2,1,0:T(8,128)(2,1)S(1)} %shard_map.49), channel_id=1, replica_groups=mesh['dom'=32,'feat'=8] {'dom'}, dimensions={0} | all-to-all | bytes 3670016 | tf_op jit(solution)/shard_map/all_to_all | solution.py:162
  153.3 0.0 copy-done.1
  153.3 1.1 shard_map.50
  154.4 48.7 %all_to_all.44.windows = bf16[32,32,896]{2,1,0:T(8,128)(2,1)S(1)} all-to-all(bf16[32,32,896]{2,1,0:T(8,128)(2,1)S(1)} %get-tuple-element.16), channel_id=1, replica_groups=mesh['dom'=32,'feat'=8] {'dom'}, dimensions={0} | all-to-all | bytes 3670016 | tf_op jit(solution)/shard_map/all_to_all | solution.py:162
  203.1 8.3 %shard_map.51 = f32[8,32,256]{2,1,0:T(8,128)S(1)} custom-call(bf16[32,32,896]{2,1,0:T(8,128)(2,1)S(1)} %all_to_all.44.windows, bf16[256,25088]{1,0:T(8,128)(2,1)} %bitcast.10), custom_call_target="tpu_custom_call" | custom-call | tf_op jit(solution)/shard_map/pallas_call | solution.py:185
  211.4 9.9 %all_to_all.45.partials = f32[8,32,256]{2,1,0:T(8,128)S(1)} all-to-all(f32[8,32,256]{2,1,0:T(8,128)S(1)} %shard_map.51), channel_id=1, replica_groups=mesh['dom'=32,'feat'=8] {'feat'}, dimensions={0} | all-to-all | bytes 524288 | tf_op jit(solution)/shard_map/all_to_all | solution.py:162
  221.3 0.8 shard_map.52
  222.1 14.2 %all_to_all.46.grams = f32[32,8,128]{2,1,0:T(8,128)S(1)} all-to-all(f32[32,8,128]{2,1,0:T(8,128)S(1)} %get-tuple-element.17), channel_id=1, replica_groups=mesh['dom'=32,'feat'=8] {'dom'}, dimensions={0} | all-to-all | bytes 262144 | tf_op jit(solution)/shard_map/all_to_all | solution.py:162
  236.3 9.7 %shard_map.53 = bf16[32,32,896]{2,1,0:T(8,128)(2,1)S(1)} custom-call(f32[32,8,128]{2,1,0:T(8,128)S(1)} %all_to_all.46.grams, f32[32,256]{1,0:T(8,128)S(1)} %get-tuple-element.18.own, f32[32,256]{1,0:T(8,128)S(1)} %get-tuple-element.19.partner, bf16[256,25088]{1,0:T(8,128)(2,1)} %bitcast.11), custom_call_target="tpu_custom_call" | custom-call | tf_op jit(solution)/shard_map/pallas_call | solution.py:197
  246.0 48.3 %all_to_all.47.windows = bf16[32,32,896]{2,1,0:T(8,128)(2,1)S(1)} all-to-all(bf16[32,32,896]{2,1,0:T(8,128)(2,1)S(1)} %shard_map.53), channel_id=1, replica_groups=mesh['dom'=32,'feat'=8] {'dom'}, dimensions={0} | all-to-all | bytes 3670016 | tf_op jit(solution)/shard_map/all_to_all | solution.py:162
  294.4 1.5 shard_map.54
Async XLA Ops:
  2.1 0.9 copy-start
  104.8 48.5 %copy-start.1 = (f32[1,32,784]{2,1,0:T(8,128)S(1)}, f32[1,32,784]{2,1,0:T(8,128)}, u32[]{:S(2)}) copy-start(f32[1,32,784]{2,1,0:T(8,128)} %param.5) | copy-start | bytes 301060
